TPU v7x, 32 devices: a whole 2x2x4 slice. The times are simulated.
32 devices in a mesh: dp: 4 (over z), tensor: 4 (over y, x), adapter: 2 (over core).
Axes of the slice: x: 2, y: 2, z: 4, core: 2. Of those that a mesh axis runs over, the one named last changes fastest.
Arguments:
- tokens: bfloat16 [4096, 8192], P('dp', 'tensor'), may hold values from -6 to 6
- frozen_weight: bfloat16 [8192, 2048], P(None, 'tensor'), may hold values from -0.0625 to 0.0625
- adapter_down_weight: bfloat16 [64, 64, 8192], P('adapter', None, 'tensor'), may hold values from -0.0625 to 0.0625
- adapter_up_weight: bfloat16 [64, 64, 2048], P('adapter', None, 'tensor'), may hold values from -0.75 to 0.75
- output_cotangent: bfloat16 [4096, 2048], P('dp', 'tensor'), may hold values from -6 to 6
- principle_per_block: int32 [32], P('dp'), may hold values from 0 to 63
- live_block_rows: int32 [32], P('dp'), may hold values from 16 to 128, as said below
Outputs:
- adapted_output: bfloat16 [4096, 2048], P('dp', 'tensor')
- hidden_input_gradient: bfloat16 [4096, 8192], P('dp', 'tensor')
- down_map_gradient: float32 [64, 64, 8192], P('adapter', 'dp', 'tensor')
- up_map_gradient: float32 [64, 64, 2048], P('adapter', 'dp', 'tensor')
Inputs may be any that keep to these rules, and one draw needn't show every extreme that they name: `live_block_rows`: between 16 and 128; the first block of each index of dp is full.
All inputs are finite; a program needn't handle non-finite values.
Results may differ from a plain program's by a relative error of at most 0.014.
Values may be sent and summed in bfloat16 or wider, within the bound.
A program may use at most 192 MiB of HBM per device.

v0:
```python
import jax
import jax.numpy as jnp
from jax import lax
from jax.sharding import PartitionSpec as P

BLOCK = 128


ADAPTER_SCALE = 2.0


def on_device(
    tokens,
    frozen_weight,
    adapter_down_weight,
    adapter_up_weight,
    output_cotangent,
    principle_per_block,
    live_block_rows,
):
    token_rows, local_feature_width = tokens.shape
    output_feature_width = frozen_weight.shape[1]
    rows_per_group = adapter_down_weight.shape[0]
    num_blocks = token_rows // BLOCK
    core_index = lax.axis_index("adapter")
    slot_ids = jnp.arange(rows_per_group, dtype=jnp.int32)
    local_pick = principle_per_block - core_index * rows_per_group
    owned = (local_pick >= 0) & (local_pick < rows_per_group)
    selected_adapter = jnp.clip(local_pick, 0, rows_per_group - 1)
    within = jnp.arange(BLOCK, dtype=jnp.int32)
    row_mask = ((within[None, :] < live_block_rows[:, None]) & owned[:, None]).astype(jnp.float32)[
        :, :, None
    ]
    selected_down_weight = jnp.take(adapter_down_weight, selected_adapter, axis=0)
    selected_up_weight = jnp.take(adapter_up_weight, selected_adapter, axis=0)
    padded_token_blocks = tokens.reshape(num_blocks, BLOCK, local_feature_width)
    gradient_token_blocks = output_cotangent.reshape(num_blocks, BLOCK, output_feature_width)
    down_part = (
        jnp.einsum(
            "avc,amc->avm",
            padded_token_blocks,
            selected_down_weight,
            preferred_element_type=jnp.float32,
        )
        * row_mask
    )
    back_part = (
        jnp.einsum(
            "brc,bkc->brk",
            gradient_token_blocks,
            selected_up_weight,
            preferred_element_type=jnp.float32,
        )
        * row_mask
    )
    rank_projected_hidden, backrank = (
        lax.psum(down_part.astype(jnp.bfloat16), "tensor").astype(jnp.float32),
        lax.psum(back_part.astype(jnp.bfloat16), "tensor").astype(jnp.float32),
    )
    block_rank_state = rank_projected_hidden.astype(jnp.bfloat16)
    backward_block_rows = backrank.astype(jnp.bfloat16)
    adapter_output_delta = ADAPTER_SCALE * jnp.einsum(
        "xyl,xlp->xyp", block_rank_state, selected_up_weight, preferred_element_type=jnp.float32
    )
    adapter_input_gradient = ADAPTER_SCALE * jnp.einsum(
        "vis,vsy->viy",
        backward_block_rows,
        selected_down_weight,
        preferred_element_type=jnp.float32,
    )
    adapter_output_delta, adapter_input_gradient = (
        lax.psum(
            adapter_output_delta.reshape(token_rows, output_feature_width).astype(jnp.bfloat16),
            "adapter",
        ).astype(jnp.float32),
        lax.psum(
            adapter_input_gradient.reshape(token_rows, local_feature_width).astype(jnp.bfloat16),
            "adapter",
        ).astype(jnp.float32),
    )
    weight_rows = frozen_weight
    frozen_output = jnp.dot(
        lax.all_gather(tokens, "tensor", axis=1, tiled=True),
        weight_rows,
        preferred_element_type=jnp.float32,
    )
    weight_rows = frozen_weight
    frozen_input_grad = (
        lax.psum_scatter(
            lax.dot_general(
                weight_rows,
                output_cotangent,
                (((1,), (1,)), ((), ())),
                preferred_element_type=jnp.float32,
            ).astype(jnp.bfloat16),
            "tensor",
            scatter_dimension=0,
            tiled=True,
        )
        .astype(jnp.float32)
        .T
    )
    adapted_output = (frozen_output + adapter_output_delta).astype(jnp.bfloat16)
    hidden_input_gradient = (frozen_input_grad + adapter_input_gradient).astype(jnp.bfloat16)
    principle_selector = ((selected_adapter[:, None] == slot_ids[None, :]) & owned[:, None]).astype(
        jnp.float32
    )
    down_block_weight = ADAPTER_SCALE * jnp.einsum(
        "szj,szy->sjy", backward_block_rows, padded_token_blocks, preferred_element_type=jnp.float32
    )
    up_block_weight = ADAPTER_SCALE * jnp.einsum(
        "vwf,vwh->vfh", block_rank_state, gradient_token_blocks, preferred_element_type=jnp.float32
    )
    down_block_local = jnp.einsum(
        "eh,ecm->hcm", principle_selector, down_block_weight, precision=lax.Precision.HIGHEST
    )
    up_local = jnp.einsum(
        "bp,bkc->pkc", principle_selector, up_block_weight, precision=lax.Precision.HIGHEST
    )
    down_map_gradient, up_map_gradient = (
        lax.psum_scatter(
            down_block_local.astype(jnp.bfloat16), "dp", scatter_dimension=1, tiled=True
        ).astype(jnp.float32),
        lax.psum_scatter(
            up_local.astype(jnp.bfloat16), "dp", scatter_dimension=1, tiled=True
        ).astype(jnp.float32),
    )
    return (adapted_output, hidden_input_gradient, down_map_gradient, up_map_gradient)


def solution(mesh):
    in_specs = (
        P("dp", "tensor"),
        P(None, "tensor"),
        P("adapter", None, "tensor"),
        P("adapter", None, "tensor"),
        P("dp", "tensor"),
        P("dp"),
        P("dp"),
    )
    out_specs = (
        P("dp", "tensor"),
        P("dp", "tensor"),
        P("adapter", "dp", "tensor"),
        P("adapter", "dp", "tensor"),
    )
    return jax.shard_map(
        on_device, mesh=mesh, in_specs=in_specs, out_specs=out_specs, check_vma=False
    )
```

profile of v0, /device:TPU:0, one launch (start us, length us, event | category | flops | bytes accessed | tf_op | source)
XLA Modules:
  0.0 633.7 jit_solution(14732662327186183117)
XLA Ops:
  7.2 0.8 compare_and_fusion.1
  8.1 5.4 gather_fusion
  13.4 0.6 gather_fusion.1
  14.1 0.1 fusion.8
  14.1 5.2 fusion.4
  19.3 1.2 fusion.5
  20.5 0.0 reduce-scatter.8.cloned.1.call-start
  20.5 45.9 %all-reduce.5.cloned.1.call-done = (bf16[8,128,64]{1,2,0:T(8,128)(2,1)}, bf16[8,128,64]{1,2,0:T(8,128)(2,1)}) async-done(((bf16[8,128,64]{1,2,0:T(8,128)(2,1)}, bf16[8,128,64]{1,2,0:T(8,128)(2,1)}), (bf16[8,128,64]{1,2,0:T(8,128)(2,1)}, bf16[8,128,64]{1,2,0:T(8,128)(2,1)})) %all-reduce.5.cloned.1.call-update) | async-done | bytes 262160 | tf_op jit(solution)/shard_map/psum | solution.py:58
  66.4 1.2 fusion.24
  67.7 3.2 convolution_convert_fusion.2
  70.9 0.0 reduce-scatter.6.cloned.1.call-start
  71.0 2.9 fusion.23
  73.9 9.3 %convolution_convert_fusion.1 = bf16[32,64,2048]{2,0,1:T(8,128)(2,1)} fusion(f32[8,64,2048]{2,1,0:T(8,128)S(1)} %fusion.23, s32[8]{0:T(128)S(1)} %get-tuple-element.13, pred[8]{0:T(512)(128)(4,1)S(1)} %get-tuple-element.14), kind=kOutput, calls=%fused_computation.6 | convolution fusion | flops 407896576 | bytes 12582952 | tf_op jit(solution)/shard_map/eh,ecm->hcm/dot_general | solution.py:114
  83.2 0.0 all-reduce.7.cloned.1.call-start
  83.3 1.6 copy-done.2
  84.8 3.3 multiply_convert_fusion
  88.1 6.4 %copy.17 = bf16[1024,2048]{0,1:T(8,128)(2,1)} copy(bf16[1024,2048]{1,0:T(8,128)(2,1)} %bitcast.30) | data formatting | bytes 8388608 | tf_op jit(solution)/shard_map/convert_element_type | solution.py:77
  94.6 1.5 multiply_convert_fusion.1
  96.1 0.5 all-gather.2.cloned.1.call-update
  96.7 0.2 reduce-scatter.4.cloned.1.call-start
  96.9 0.4 copy-done.4
  97.3 16.0 %convolution_convert_fusion = bf16[8192,1024]{1,0:T(8,128)(2,1)} fusion(bf16[8192,512]{1,0:T(8,128)(2,1)} %param.8, bf16[1024,512]{1,0:T(8,128)(2,1)S(1)} %copy-done.4), kind=kOutput, calls=%fused_computation.2 | convolution fusion | flops 8598323200 | bytes 26214400 | tf_op jit(solution)/shard_map/dot_general | solution.py:90
  113.3 1.7 reduce-scatter.8.cloned.1.call-done
  115.0 2.3 copy.14
  117.3 143.9 %reduce-scatter.6.cloned.1.call-done = bf16[32,16,2048]{2,0,1:T(8,128)(2,1)} async-done(((bf16[32,64,2048]{2,0,1:T(8,128)(2,1)}), bf16[32,16,2048]{2,0,1:T(8,128)(2,1)}) %reduce-scatter.6.cloned.1.call-update) | async-done | bytes 2097168 | tf_op jit(solution)/shard_map/reduce_scatter | solution.py:121
  261.2 4.8 copy.13
  266.1 29.1 %all-reduce.7.cloned.1.call-done = (bf16[1024,512]{1,0:T(8,128)(2,1)}, bf16[1024,2048]{0,1:T(8,128)(2,1)}) async-done(((bf16[1024,512]{1,0:T(8,128)(2,1)}, bf16[1024,2048]{0,1:T(8,128)(2,1)}), (bf16[1024,512]{1,0:T(8,128)(2,1)}, bf16[1024,2048]{0,1:T(8,128)(2,1)})) %all-reduce.7.cloned.1.call-update) | async-done | bytes 5242896 | tf_op jit(solution)/shard_map/psum | solution.py:72
  295.2 160.5 %all-gather.2.cloned.1.call-done = bf16[1024,8192]{1,0:T(8,128)(2,1)} async-done(((bf16[1024,2048]{1,0:T(8,128)(2,1)}), bf16[1024,8192]{1,0:T(8,128)(2,1)}) %all-gather.2.cloned.1.call-update) | async-done | bytes 16777232 | tf_op jit(solution)/shard_map/all_gather | solution.py:83
  455.6 15.7 %add_convert_fusion = bf16[1024,512]{1,0:T(8,128)(2,1)} fusion(bf16[1024,512]{1,0:T(8,128)(2,1)} %get-tuple-element.10, bf16[1024,8192]{1,0:T(8,128)(2,1)} %all-gather.2.cloned.1.call-done, bf16[8192,512]{1,0:T(8,128)(2,1)} %param.8), kind=kOutput, calls=%fused_computation.9 | convolution fusion | flops 8591507456 | bytes 27262976 | tf_op jit(solution)/shard_map/dot_general | solution.py:82
  471.3 141.4 %reduce-scatter.4.cloned.1.call-done = bf16[2048,1024]{1,0:T(8,128)(2,1)} async-done(((bf16[8192,1024]{1,0:T(8,128)(2,1)}), bf16[2048,1024]{1,0:T(8,128)(2,1)}) %reduce-scatter.4.cloned.1.call-update) | async-done | bytes 4194320 | tf_op jit(solution)/shard_map/reduce_scatter | solution.py:89
  612.7 7.7 %fusion = bf16[1024,2048]{0,1:T(8,128)(2,1)} fusion(bf16[2048,1024]{1,0:T(8,128)(2,1)} %reduce-scatter.4.cloned.1.call-done, bf16[1024,2048]{0,1:T(8,128)(2,1)} %get-tuple-element.11), kind=kLoop, calls=%fused_computation.4 | loop fusion | flops 8388608 | bytes 12582912 | tf_op jit(solution)/shard_map/convert_element_type | solution.py:104
  620.4 6.4 %copy.12 = bf16[1024,2048]{1,0:T(8,128)(2,1)} copy(bf16[1024,2048]{0,1:T(8,128)(2,1)} %fusion) | data formatting | bytes 8388608
  (23 shorter events, 0.2 us)
Async XLA Ops:
  7.2 6.3 copy-start
  7.2 6.9 %copy-start.7 = (s32[8]{0:T(128)S(1)}, s32[8]{0:T(128)}, u32[]{:S(2)}) copy-start(s32[8]{0:T(128)} %param.13) | copy-start | bytes 100
  7.2 59.2 %all-reduce.5.cloned.1.call-start = ((), (), s32[]{:S(2)}) async-start(), calls=%async_computation.7 | async-start | bytes 524288 | tf_op jit(solution)/shard_map/psum | solution.py:58
  14.0 5.3 copy-start.3
  20.5 94.5 %reduce-scatter.8.cloned.1.call-start = ((), (), s32[]{:S(2)}) async-start(), calls=%async_computation.6 | async-start | bytes 2621440 | tf_op jit(solution)/shard_map/reduce_scatter | solution.py:124
  66.4 4.5 copy-start.5
  70.9 190.3 %reduce-scatter.6.cloned.1.call-start = ((), (), s32[]{:S(2)}) async-start(), calls=%async_computation.5 | async-start | bytes 10485760 | tf_op jit(solution)/shard_map/reduce_scatter | solution.py:121
  83.2 1.6 copy-start.2
  83.2 212.0 %all-reduce.7.cloned.1.call-start = ((), (), s32[]{:S(2)}) async-start(), calls=%async_computation.8 | async-start | bytes 10485760 | tf_op jit(solution)/shard_map/psum | solution.py:72
  88.1 6.4 %copy-start.6 = (bf16[8,128,64]{1,2,0:T(8,128)(2,1)S(1)}, bf16[8,128,64]{1,2,0:T(8,128)(2,1)}, u32[]{:S(2)}) copy-start(bf16[8,128,64]{1,2,0:T(8,128)(2,1)} %get-tuple-element.9) | copy-start | bytes 393220
  96.0 1.2 copy-start.4
  96.1 359.6 %all-gather.2.cloned.1.call-start = ((), (), s32[]{:S(2)}) async-start(), calls=%async_computation.3 | async-start | bytes 20971520 | tf_op jit(solution)/shard_map/all_gather | solution.py:83
  96.7 516.1 %reduce-scatter.4.cloned.1.call-start = ((), (), s32[]{:S(2)}) async-start(), calls=%async_computation.4 | async-start | bytes 20971520 | tf_op jit(solution)/shard_map/reduce_scatter | solution.py:89
  612.7 14.1 %copy-start.1 = (bf16[32,64,512]{2,1,0:T(8,128)(2,1)S(1)}, bf16[32,64,512]{2,1,0:T(8,128)(2,1)}, u32[]{:S(2)}) copy-start(bf16[32,64,512]{2,1,0:T(8,128)(2,1)} %param.10) | copy-start | bytes 6291460
Sparse Core Ops, SparseCore 0:
  20.6 45.7 all-reduce.4
  71.0 43.9 reduce-scatter.7
  117.4 143.8 reduce-scatter.5
  264.2 30.9 all-reduce.6
  297.0 158.5 all-gather.1
  458.9 153.8 reduce-scatter.3
where the time goes:
time: 634 us
  waiting for transfers between devices  523 us (82%)
  matrix products  59.4 us (9%)
  local copies, waits for them, and re-layouts  27.9 us (4%)
  between operations  14.2 us (2%)
  other arithmetic  8.56 us (1%)
    all_gather x1, waiting for transfers between devices, on_device(): lax.all_gather(tokens, 'tensor', axis=1, tiled=True)  160 us
    reduce_scatter x1, waiting for transfers between devices, on_device(): lax.psum_scatter(down_block_local.astype(jnp.bfloat16), 'dp', scatter_dim...  144 us
    reduce_scatter x1, waiting for transfers between devices, on_device(): lax.psum_scatter(lax.dot_general(weight_rows, output_cotangent, (((1,), (...  141 us
    psum x1, waiting for transfers between devices, on_device(): lax.psum(back_part.astype(jnp.bfloat16), 'tensor').astype(jnp.float32)  45.9 us
    psum x1, waiting for transfers between devices, on_device(): lax.psum(adapter_output_delta.reshape(token_rows, output_feature_width).a...  29.1 us
    dot_general x1, matrix products, on_device(): lax.dot_general(weight_rows, output_cotangent, (((1,), (1,)), ((), ())),...  16 us
    dot_general x1, matrix products, on_device(): jnp.dot(lax.all_gather(tokens, 'tensor', axis=1, tiled=True), weight_rows...  15.7 us
    unnamed x19, local copies, waits for them, and re-layouts  15.5 us
  transfers between devices with their start and end apart: 6, of which 6 were waited for; matrix products, arithmetic and copies ran while one was open for 10% of the time, Pallas kernels for 0%

commit v1 on v0

v1 whole, which is shorter than its diff:
```python
import functools

import jax
import jax.numpy as jnp
from jax import lax
from jax.experimental import pallas as pl
from jax.experimental.pallas import tpu as pltpu
from jax.sharding import PartitionSpec as P

BLOCK = 128
ADAPTER_SCALE = 2.0
MESH = pl.DeviceIdType.MESH


def flip(index, distance, count):
    out, bit = 0, 1
    while bit < count:
        out = out + ((index // bit + distance // bit) % 2) * bit
        bit *= 2
    return out


def tile_of(size, most):
    return most if size % most == 0 else size


def kernel(
    num_tensor,
    num_dp,
    tok_ref,
    w_ref,
    down_ref,
    up_ref,
    cot_ref,
    pick_ref,
    own_ref,
    live_ref,
    ids_ref,
    out_ref,
    hid_ref,
    gd_ref,
    gu_ref,
    gid_ref,
    tok_v,
    wf,
    cotf,
    down_v,
    up_v,
    a_snd,
    a_rcv,
    a_own,
    b_snd,
    b_rcv,
    b_own,
    rk_snd,
    rk_rcv,
    rank_v,
    gd_snd,
    gu_snd,
    acc,
    o_zero,
    o_snd,
    o_rcv,
    o_fin,
    h_fin,
    loc_sem,
    cot_s,
    cot_r,
    w_s,
    w_r,
    wr_s,
    wr_r,
    ab_s,
    ab_r,
    rk_s,
    rk_r,
    g_s,
    g_r,
    gr_s,
    gr_r,
    o_s,
    o_r,
    fin_s,
    fin_r,
):
    z = lax.axis_index("dp")
    t = lax.axis_index("tensor")
    a = lax.axis_index("adapter")
    pa = 1 - a
    rows, d = tok_v.shape
    c = cotf.shape[2]
    half = d // 2
    nb = rows // BLOCK
    rank = down_v.shape[1]
    rk = rank // num_dp
    partner = (z, t, pa)
    my_rows = pl.ds(pl.multiple_of(a * rows, rows), rows)
    my_half = pl.ds(pl.multiple_of(a * half, half), half)

    def local(src, dst, sem):
        copy = pltpu.make_async_copy(src, dst, loc_sem.at[sem])
        copy.start()
        return copy

    def remote(src, dst, ss, rs, dev):
        copy = pltpu.make_async_remote_copy(
            src_ref=src, dst_ref=dst, send_sem=ss, recv_sem=rs, device_id=dev, device_id_type=MESH
        )
        copy.start()
        return copy

    cp_cot = local(cot_ref.at[my_rows, :], cotf.at[0], 0)
    cp_down = local(down_ref, down_v, 1)
    cp_up = local(up_ref, up_v, 2)
    cp_tok = local(tok_ref.at[my_rows, :], tok_v, 3)
    cp_w = local(w_ref.at[pl.ds(pl.multiple_of(t * d, d), d), :], wf.at[0], 4)

    tensor_peer = [None] + [(z, flip(t, k, num_tensor), a) for k in range(1, num_tensor)]
    dp_peer = [None] + [(lax.rem(z + j, num_dp), t, a) for j in range(1, num_dp)]
    barrier = pltpu.get_barrier_semaphore()
    for peer in tensor_peer[1:] + dp_peer[1:] + [partner]:
        pl.semaphore_signal(barrier, inc=1, device_id=peer, device_id_type=MESH)
    pl.semaphore_wait(barrier, num_tensor + num_dp - 1)

    cot_c, w_c = [None], [None]
    for k in range(1, num_tensor):
        cot_c.append(
            remote(cot_ref.at[my_rows, :], cotf.at[k], cot_s.at[k], cot_r.at[k], tensor_peer[k])
        )
    for k in range(1, num_tensor):
        start = pl.multiple_of(tensor_peer[k][1] * d + a * half, half)
        w_c.append(
            remote(
                w_ref.at[pl.ds(start, half), :],
                wf.at[k, my_half, :],
                w_s.at[k],
                w_r.at[k],
                tensor_peer[k],
            )
        )

    cp_down.wait()
    cp_up.wait()
    for i in range(nb):
        b = pa * nb + i
        a_snd[i] = (down_v[pick_ref[b]].astype(jnp.float32) * own_ref[b]).astype(jnp.bfloat16)
        b_snd[i] = (up_v[pick_ref[b]].astype(jnp.float32) * own_ref[b]).astype(jnp.bfloat16)
    a_c = remote(a_snd, a_rcv, ab_s.at[0], ab_r.at[0], partner)
    b_c = remote(b_snd, b_rcv, ab_s.at[1], ab_r.at[1], partner)
    for i in range(nb):
        b = a * nb + i
        a_own[i] = (down_v[pick_ref[b]].astype(jnp.float32) * own_ref[b]).astype(jnp.bfloat16)
        b_own[i] = (up_v[pick_ref[b]].astype(jnp.float32) * own_ref[b]).astype(jnp.bfloat16)
    a_c.wait_recv()
    b_c.wait_recv()
    for i in range(nb):
        a_own[i] = a_own[i] + a_rcv[i]
        b_own[i] = b_own[i] + b_rcv[i]

    cp_tok.wait()
    cp_cot.wait()
    last = (((1,), (1,)), ((), ()))
    for i in range(nb):
        blk = slice(i * BLOCK, (i + 1) * BLOCK)
        low = lax.dot_general(tok_v[blk, :], a_own[i], last, preferred_element_type=jnp.float32)
        back = lax.dot_general(cotf[0, blk, :], b_own[i], last, preferred_element_type=jnp.float32)
        rk_snd[blk, :] = jnp.concatenate([low, back], axis=1).astype(jnp.bfloat16)
    rk_c = [None]
    for k in range(1, num_tensor):
        rk_c.append(remote(rk_snd, rk_rcv.at[k], rk_s.at[k], rk_r.at[k], tensor_peer[k]))

    row_tile = tile_of(rows, 256)
    d_tile = tile_of(d, 512)

    def forward(k, store):
        @pl.loop(0, rows // row_tile)
        def _(step):
            at = pl.ds(pl.multiple_of(step * row_tile, row_tile), row_tile)
            store(at, jnp.dot(tok_v[at, :], wf[k], preferred_element_type=jnp.float32))

    def backward(k):
        @pl.loop(0, d // d_tile)
        def _(step):
            at = pl.ds(pl.multiple_of(step * d_tile, d_tile), d_tile)
            part = lax.dot_general(cotf[k], wf[k, at, :], last, preferred_element_type=jnp.float32)
            part = part.astype(jnp.bfloat16).astype(jnp.float32)
            acc[:, at] = part if k == 0 else acc[:, at] + part

    def store_zero(at, value):
        o_zero[at, :] = value

    cp_w.wait()
    forward(0, store_zero)
    backward(0)

    for k in range(1, num_tensor):
        rk_c[k].wait_recv()
    within = lax.broadcasted_iota(jnp.int32, (BLOCK, 2 * rank), 0)
    for i in range(nb):
        blk = slice(i * BLOCK, (i + 1) * BLOCK)
        total = rk_snd[blk, :].astype(jnp.float32)
        for k in range(1, num_tensor):
            total = total + rk_rcv[k, blk, :].astype(jnp.float32)
        total = jnp.where(within < live_ref[a * nb + i], total, 0.0)
        rank_v[blk, :] = total.astype(jnp.bfloat16)
        turned = total.T.astype(jnp.bfloat16)
        gd = jnp.dot(turned[rank:], tok_v[blk, :], preferred_element_type=jnp.float32)
        gu = jnp.dot(turned[:rank], cotf[0, blk, :], preferred_element_type=jnp.float32)
        gd = ADAPTER_SCALE * gd
        gu = ADAPTER_SCALE * gu
        for j in range(num_dp):
            part = slice(i * rk, (i + 1) * rk)
            gd_snd[j, part, :] = gd[j * rk : (j + 1) * rk].astype(jnp.bfloat16)
            gu_snd[j, part, :] = gu[j * rk : (j + 1) * rk].astype(jnp.bfloat16)
    g_c = [None]
    for j in range(1, num_dp):
        to = dp_peer[j][0]
        g_c.append(
            (
                remote(gd_snd.at[to], gd_ref.at[z, a], g_s.at[0, j], g_r.at[0, j], dp_peer[j]),
                remote(gu_snd.at[to], gu_ref.at[z, a], g_s.at[1, j], g_r.at[1, j], dp_peer[j]),
                remote(ids_ref, gid_ref.at[z], g_s.at[2, j], g_r.at[2, j], dp_peer[j]),
            )
        )
    cp_gd = local(gd_snd.at[z], gd_ref.at[z, a], 5)
    cp_gu = local(gu_snd.at[z], gu_ref.at[z, a], 6)
    cp_id = local(ids_ref, gid_ref.at[z], 7)
    gr_c = [
        (
            remote(gd_snd.at[z], gd_ref.at[z, a], gr_s.at[0, 0], gr_r.at[0, 0], partner),
            remote(gu_snd.at[z], gu_ref.at[z, a], gr_s.at[1, 0], gr_r.at[1, 0], partner),
        )
    ]

    wr_c = [None] * num_tensor
    o_c = [None] * num_tensor

    def relay(k):
        w_c[k].wait_recv()
        wr_c[k] = remote(
            wf.at[k, my_half, :], wf.at[k, my_half, :], wr_s.at[k], wr_r.at[k], partner
        )

    relay(1)
    for k in range(1, num_tensor):
        if k + 1 < num_tensor and k < 2:
            relay(k + 1)
        wr_c[k].wait_recv()

        def store_send(at, value, k=k):
            o_snd[k, at, :] = value.astype(jnp.bfloat16)

        forward(k, store_send)
        o_c[k] = remote(o_snd.at[k], o_rcv.at[k], o_s.at[k], o_r.at[k], tensor_peer[k])
        if k >= 2 and k + 1 < num_tensor:
            relay(k + 1)
        cot_c[k].wait_recv()
        backward(k)

    for i in range(nb):
        blk = slice(i * BLOCK, (i + 1) * BLOCK)
        low_b = rank_v[blk, :rank]
        back_b = rank_v[blk, rank:]
        term = jnp.dot(back_b, a_own[i], preferred_element_type=jnp.float32)
        h_fin[blk, :] = (acc[blk, :] + ADAPTER_SCALE * term).astype(jnp.bfloat16)
        o_term = jnp.dot(low_b, b_own[i], preferred_element_type=jnp.float32)
        o_zero[blk, :] = o_zero[blk, :] + ADAPTER_SCALE * o_term
    h_c = remote(h_fin, hid_ref.at[my_rows, :], fin_s.at[0], fin_r.at[0], partner)
    cp_h = local(h_fin, hid_ref.at[my_rows, :], 8)

    for j in range(1, num_dp):
        for copy in g_c[j]:
            copy.wait_recv()
        source = lax.rem(z + num_dp - j, num_dp)
        mine_d, mine_u = gd_ref.at[source, a], gu_ref.at[source, a]
        gr_c.append(
            (
                remote(mine_d, mine_d, gr_s.at[0, j], gr_r.at[0, j], partner),
                remote(mine_u, mine_u, gr_s.at[1, j], gr_r.at[1, j], partner),
            )
        )

    for k in range(1, num_tensor):
        o_c[k].wait_recv()
    for i in range(nb):
        blk = slice(i * BLOCK, (i + 1) * BLOCK)
        total = o_zero[blk, :]
        for k in range(1, num_tensor):
            total = total + o_rcv[k, blk, :].astype(jnp.float32)
        o_fin[blk, :] = total.astype(jnp.bfloat16)
    of_c = remote(o_fin, out_ref.at[my_rows, :], fin_s.at[1], fin_r.at[1], partner)
    cp_o = local(o_fin, out_ref.at[my_rows, :], 9)

    for copy in (cp_gd, cp_gu, cp_id, cp_h, cp_o):
        copy.wait()
    for k in range(1, num_tensor):
        cot_c[k].wait_send()
        w_c[k].wait_send()
        rk_c[k].wait_send()
        wr_c[k].wait_send()
        o_c[k].wait_send()
    a_c.wait_send()
    b_c.wait_send()
    for j in range(1, num_dp):
        for copy in g_c[j]:
            copy.wait_send()
    for pair in gr_c:
        for copy in pair:
            copy.wait()
    h_c.wait()
    of_c.wait()


def on_device(
    num_tensor,
    num_dp,
    tokens,
    frozen_weight,
    adapter_down_weight,
    adapter_up_weight,
    output_cotangent,
    principle_per_block,
    live_block_rows,
):
    all_rows, d = tokens.shape
    c = frozen_weight.shape[1]
    principles, rank = adapter_down_weight.shape[:2]
    blocks = all_rows // BLOCK
    rows, nb, rk = all_rows // 2, blocks // 2, rank // num_dp
    core = lax.axis_index("adapter")
    local_pick = principle_per_block - core * principles
    owned = ((local_pick >= 0) & (local_pick < principles)).astype(jnp.float32)
    pick = jnp.clip(local_pick, 0, principles - 1)
    ids = jnp.broadcast_to(principle_per_block.astype(jnp.float32)[:, None], (blocks, 128))

    bf, f32 = jnp.bfloat16, jnp.float32
    hbm = pl.BlockSpec(memory_space=pl.ANY)
    smem = pl.BlockSpec(memory_space=pltpu.SMEM)
    dma = pltpu.SemaphoreType.DMA
    T, Z = num_tensor, num_dp
    out, hidden, gd, gu, gid = pl.pallas_call(
        functools.partial(kernel, T, Z),
        out_shape=(
            jax.ShapeDtypeStruct((all_rows, c), bf),
            jax.ShapeDtypeStruct((all_rows, d), bf),
            jax.ShapeDtypeStruct((Z, 2, nb * rk, d), bf),
            jax.ShapeDtypeStruct((Z, 2, nb * rk, c), bf),
            jax.ShapeDtypeStruct((Z, blocks, 128), f32),
        ),
        in_specs=[hbm] * 5 + [smem] * 3 + [hbm],
        out_specs=[hbm] * 5,
        scratch_shapes=[
            pltpu.VMEM((rows, d), bf),
            pltpu.VMEM((T, d, c), bf),
            pltpu.VMEM((T, rows, c), bf),
            pltpu.VMEM((principles, rank, d), bf),
            pltpu.VMEM((principles, rank, c), bf),
            pltpu.VMEM((nb, rank, d), bf),
            pltpu.VMEM((nb, rank, d), bf),
            pltpu.VMEM((nb, rank, d), bf),
            pltpu.VMEM((nb, rank, c), bf),
            pltpu.VMEM((nb, rank, c), bf),
            pltpu.VMEM((nb, rank, c), bf),
            pltpu.VMEM((rows, 2 * rank), bf),
            pltpu.VMEM((T, rows, 2 * rank), bf),
            pltpu.VMEM((rows, 2 * rank), bf),
            pltpu.VMEM((Z, nb * rk, d), bf),
            pltpu.VMEM((Z, nb * rk, c), bf),
            pltpu.VMEM((rows, d), f32),
            pltpu.VMEM((rows, c), f32),
            pltpu.VMEM((T, rows, c), bf),
            pltpu.VMEM((T, rows, c), bf),
            pltpu.VMEM((rows, c), bf),
            pltpu.VMEM((rows, d), bf),
            dma((10,)),
            dma((T,)),
            dma((T,)),
            dma((T,)),
            dma((T,)),
            dma((T,)),
            dma((T,)),
            dma((2,)),
            dma((2,)),
            dma((T,)),
            dma((T,)),
            dma((3, Z)),
            dma((3, Z)),
            dma((2, Z)),
            dma((2, Z)),
            dma((T,)),
            dma((T,)),
            dma((2,)),
            dma((2,)),
        ],
        compiler_params=pltpu.CompilerParams(
            collective_id=0, has_side_effects=True, vmem_limit_bytes=56 * 1024 * 1024
        ),
        cost_estimate=pl.CostEstimate(
            flops=4 * rows * d * c * T, bytes_accessed=8 * d * c * T, transcendentals=0
        ),
    )(
        tokens,
        frozen_weight,
        adapter_down_weight,
        adapter_up_weight,
        output_cotangent,
        pick,
        owned,
        live_block_rows,
        ids,
    )
    slots = core * principles + jnp.arange(principles, dtype=jnp.int32)
    chosen = (slots[:, None].astype(f32) == gid[:, :, 0].reshape(1, -1)).astype(bf)
    gd = gd.reshape(Z * blocks, rk, d)
    gu = gu.reshape(Z * blocks, rk, c)
    down_map_gradient = jnp.einsum("pb,bkd->pkd", chosen, gd, preferred_element_type=f32)
    up_map_gradient = jnp.einsum("pb,bkd->pkd", chosen, gu, preferred_element_type=f32)
    return out, hidden, down_map_gradient, up_map_gradient


def solution(mesh):
    in_specs = (
        P("dp", "tensor"),
        P(None, "tensor"),
        P("adapter", None, "tensor"),
        P("adapter", None, "tensor"),
        P("dp", "tensor"),
        P("dp"),
        P("dp"),
    )
    out_specs = (
        P("dp", "tensor"),
        P("dp", "tensor"),
        P("adapter", "dp", "tensor"),
        P("adapter", "dp", "tensor"),
    )
    return jax.shard_map(
        functools.partial(on_device, mesh.shape["tensor"], mesh.shape["dp"]),
        mesh=mesh,
        in_specs=in_specs,
        out_specs=out_specs,
        check_vma=False,
    )
```

time: 634 us -> 135 us (0.21)
  waiting for transfers between devices: 523 us -> 0 us
  Pallas kernels: 0 us -> 116 us
  matrix products: 59.4 us -> 4.97 us
  local copies, waits for them, and re-layouts: 27.9 us -> 10.6 us
  between operations: 14.2 us -> 0.67 us
    reduce_scatter x3 -> x0, waiting for transfers between devices: 287 us -> none  [the longest x1 144 us: on_device(): lax.psum_scatter(down_block_local.astype(jnp.bfloat16), 'dp', scatter_dim...]
    all_gather x1 -> x0, waiting for transfers between devices: 160 us -> none  [on_device(): lax.all_gather(tokens, 'tensor', axis=1, tiled=True)]
    pallas_call x0 -> x1, Pallas kernels: none -> 116 us  [on_device(): pl.pallas_call(functools.partial(kernel, T, Z), out_shape=(jax.ShapeDtype...]
    psum x2 -> x0, waiting for transfers between devices: 75 us -> none  [the longest x1 45.9 us: on_device(): lax.psum(back_part.astype(jnp.bfloat16), 'tensor').astype(jnp.float32)]
    dot_general x10 -> x2, matrix products: 59.4 us -> 4.97 us  [the longest x1 4.48 us: on_device(): jnp.einsum('pb,bkd->pkd', chosen, gd, preferred_element_type=f32)]
    unnamed x19 -> x10, local copies, waits for them, and re-layouts: 15.5 us -> 9.02 us
    convert_element_type x1 -> x0, local copies, waits for them, and re-layouts: 6.44 us -> none  [on_device(): adapter_input_gradient.reshape(token_rows, local_feature_width)]
  transfers between devices with their start and end apart: 6 -> 0, of which waited for: 6 -> 0; matrix products, arithmetic and copies ran while one was open for 10% -> 0% of each run, Pallas kernels for 0% -> 0%
where the time goes in v1:
time: 135 us; the launch traced here: 134 us
  Pallas kernels  116 us (86%)
  local copies, waits for them, and re-layouts  10.6 us (8%)
  matrix products  4.97 us (4%)
  other arithmetic  2.42 us (2%)
    pallas_call x1, Pallas kernels, on_device(): pl.pallas_call(functools.partial(kernel, T, Z), out_shape=(jax.ShapeDtype...  116 us
    unnamed x10, local copies, waits for them, and re-layouts  9.02 us
    dot_general x1, matrix products, on_device(): jnp.einsum('pb,bkd->pkd', chosen, gd, preferred_element_type=f32)  4.48 us

profile of v1, /device:TPU:0, one launch (start us, length us, event | category | flops | bytes accessed | tf_op | source)
XLA Modules:
  0.0 134.5 jit_solution(2069388718985145850)
XLA Ops:
  0.6 1.2 fusion.12
  1.9 1.2 and_convert_fusion.own_ref
  3.1 0.7 broadcast_in_dim.2.ids_ref
  3.7 115.8 %shard_map.102 = (bf16[1024,512]{1,0:T(8,128)(2,1)}, bf16[1024,2048]{1,0:T(8,128)(2,1)}, bf16[4,2,64,2048]{3,2,1,0:T(8,128)(2,1)}, bf16[4,2,64,512]{3,2,1,0:T(8,128)(2,1)}, f32[4,8,128]{2,1,0:T(8,128)}) custom-call(bf16[1024,2048]{1,0:T(8,128)(2,1)} %tok_ref.1, bf16[8192,512]{1,0:T(8,128)(2,1)} %w_ref.1, bf16[32,64,2048]{2,1,0:T(8,128)(2,1)} %down_ref.1, ...), custom_call_target="tpu_custom_call" | custom-call | flops 8589934592 | bytes 33554432 | tf_op jit(solution)/shard_map/pallas_call | solution.py:341
  119.5 0.8 slice_reduce_fusion
  120.3 0.1 eq.16
  120.4 4.5 %fusion = f32[32,16,2048]{2,0,1:T(8,128)S(1)} fusion(bf16[32,16,2048]{2,1,0:T(8,128)(2,1)} %bitcast.7, f32[32]{0:T(128)S(1)} %eq.16, f32[32]{0:T(128)S(1)} %add_convert_fusion), kind=kOutput, calls=%fused_computation | convolution fusion | flops 67109888 | bytes 6291712 | tf_op jit(solution)/shard_map/pb,bkd->pkd/dot_general | solution.py:416
  124.9 0.0 copy-start.2
  124.9 0.0 copy-start.1
  124.9 4.4 %copy.17 = f32[32,16,2048]{2,1,0:T(8,128)} copy(f32[32,16,2048]{2,0,1:T(8,128)S(1)} %fusion) | data formatting | bytes 8388608
  129.4 0.0 copy-start
  129.4 0.0 copy-done.2
  129.4 0.5 fusion.2
  129.9 1.6 %copy.18 = f32[32,16,512]{2,1,0:T(8,128)} copy(f32[32,16,512]{2,0,1:T(8,128)S(1)} %fusion.2) | data formatting | bytes 2097152
  131.5 0.0 copy-done.1
  131.5 1.0 copy.25
  132.4 0.0 copy-done
  132.4 2.0 %copy.26 = bf16[1024,2048]{1,0:T(8,128)(2,1)} copy(bf16[1024,2048]{1,0:T(8,128)(2,1)S(1)} %copy-done) | data formatting | bytes 8388608
  (1 shorter events, 0.0 us)
Async XLA Ops:
  124.9 4.5 %copy-start.2 = (bf16[4,2,64,512]{3,2,1,0:T(8,128)(2,1)S(1)}, bf16[4,2,64,512]{3,2,1,0:T(8,128)(2,1)}, u32[]{:S(2)}) copy-start(bf16[4,2,64,512]{3,2,1,0:T(8,128)(2,1)} %get-tuple-element.13) | copy-start | bytes 1572868
  124.9 6.5 %copy-start.1 = (bf16[1024,512]{1,0:T(8,128)(2,1)S(1)}, bf16[1024,512]{1,0:T(8,128)(2,1)}, u32[]{:S(2)}) copy-start(bf16[1024,512]{1,0:T(8,128)(2,1)} %get-tuple-element.28) | copy-start | bytes 3145732
  129.4 3.1 %copy-start = (bf16[1024,2048]{1,0:T(8,128)(2,1)S(1)}, bf16[1024,2048]{1,0:T(8,128)(2,1)}, u32[]{:S(2)}) copy-start(bf16[1024,2048]{1,0:T(8,128)(2,1)} %get-tuple-element.29) | copy-start | bytes 12582916

commit v2 on v1

--- a/solution.py
+++ b/solution.py
@@ -32,15 +32,12 @@
     down_ref,
     up_ref,
     cot_ref,
-    pick_ref,
-    own_ref,
+    principle_ref,
     live_ref,
-    ids_ref,
     out_ref,
     hid_ref,
-    gd_ref,
-    gu_ref,
-    gid_ref,
+    dmap_ref,
+    umap_ref,
     tok_v,
     wf,
     cotf,
@@ -57,6 +54,12 @@
     rank_v,
     gd_snd,
     gu_snd,
+    ids_v,
+    gdf,
+    guf,
+    gid,
+    dmap_v,
+    umap_v,
     acc,
     o_zero,
     o_snd,
@@ -66,8 +69,12 @@
     loc_sem,
     cot_s,
     cot_r,
+    cf_s,
+    cf_r,
     w_s,
     w_r,
+    wz_s,
+    wz_r,
     wr_s,
     wr_r,
     ab_s,
@@ -91,7 +98,7 @@
     c = cotf.shape[2]
     half = d // 2
     nb = rows // BLOCK
-    rank = down_v.shape[1]
+    principles, rank = down_v.shape[:2]
     rk = rank // num_dp
     partner = (z, t, pa)
     my_rows = pl.ds(pl.multiple_of(a * rows, rows), rows)
@@ -122,35 +129,50 @@
         pl.semaphore_signal(barrier, inc=1, device_id=peer, device_id_type=MESH)
     pl.semaphore_wait(barrier, num_tensor + num_dp - 1)
 
-    cot_c, w_c = [None], [None]
-    for k in range(1, num_tensor):
-        cot_c.append(
-            remote(cot_ref.at[my_rows, :], cotf.at[k], cot_s.at[k], cot_r.at[k], tensor_peer[k])
-        )
-    for k in range(1, num_tensor):
-        start = pl.multiple_of(tensor_peer[k][1] * d + a * half, half)
-        w_c.append(
-            remote(
-                w_ref.at[pl.ds(start, half), :],
-                wf.at[k, my_half, :],
-                w_s.at[k],
-                w_r.at[k],
-                tensor_peer[k],
-            )
-        )
+    far = num_tensor - 1
+    share = half // num_dp
+    my_share = pl.ds(pl.multiple_of(a * half + z * share, share), share)
+    w_c = [None] * num_tensor
+    far_at = pl.multiple_of(tensor_peer[far][1] * d + a * half + z * share, share)
+    w_c[far] = remote(
+        w_ref.at[pl.ds(far_at, share), :],
+        wf.at[far, my_share, :],
+        w_s.at[far],
+        w_r.at[far],
+        tensor_peer[far],
+    )
+    handed = num_tensor == 4
+    cot_c = [None] * num_tensor
+    for k in range(1, far if handed else num_tensor):
+        cot_c[k] = remote(
+            cot_ref.at[my_rows, :], cotf.at[k], cot_s.at[k], cot_r.at[k], tensor_peer[k]
+        )
+
+    def chosen(table, b):
+        pick = principle_ref[b] - a * principles
+        own = jnp.where((pick >= 0) & (pick < principles), 1.0, 0.0).astype(jnp.float32)
+        pick = jnp.minimum(jnp.maximum(pick, 0), principles - 1)
+        return (table[pick].astype(jnp.float32) * own).astype(jnp.bfloat16)
 
     cp_down.wait()
     cp_up.wait()
     for i in range(nb):
-        b = pa * nb + i
-        a_snd[i] = (down_v[pick_ref[b]].astype(jnp.float32) * own_ref[b]).astype(jnp.bfloat16)
-        b_snd[i] = (up_v[pick_ref[b]].astype(jnp.float32) * own_ref[b]).astype(jnp.bfloat16)
+        a_snd[i] = chosen(down_v, pa * nb + i)
+        b_snd[i] = chosen(up_v, pa * nb + i)
     a_c = remote(a_snd, a_rcv, ab_s.at[0], ab_r.at[0], partner)
     b_c = remote(b_snd, b_rcv, ab_s.at[1], ab_r.at[1], partner)
     for i in range(nb):
-        b = a * nb + i
-        a_own[i] = (down_v[pick_ref[b]].astype(jnp.float32) * own_ref[b]).astype(jnp.bfloat16)
-        b_own[i] = (up_v[pick_ref[b]].astype(jnp.float32) * own_ref[b]).astype(jnp.bfloat16)
+        a_own[i] = chosen(down_v, a * nb + i)
+        b_own[i] = chosen(up_v, a * nb + i)
+    for b in range(2 * nb):
+        ids_v[b * rk : (b + 1) * rk, :] = jnp.full(
+            (rk, 128), principle_ref[b].astype(jnp.float32), jnp.float32
+        )
+    w_c[far].wait_recv()
+    wz_c = [None]
+    for j in range(1, num_dp):
+        mine = wf.at[far, my_share, :]
+        wz_c.append(remote(mine, mine, wz_s.at[j], wz_r.at[j], dp_peer[j]))
     a_c.wait_recv()
     b_c.wait_recv()
     for i in range(nb):
@@ -168,6 +190,29 @@
     rk_c = [None]
     for k in range(1, num_tensor):
         rk_c.append(remote(rk_snd, rk_rcv.at[k], rk_s.at[k], rk_r.at[k], tensor_peer[k]))
+    for k in range(1, far):
+        start = pl.multiple_of(tensor_peer[k][1] * d + a * half, half)
+        w_c[k] = remote(
+            w_ref.at[pl.ds(start, half), :],
+            wf.at[k, my_half, :],
+            w_s.at[k],
+            w_r.at[k],
+            tensor_peer[k],
+        )
+    cf_c = []
+    if handed:
+        for n, k in enumerate((1, 2)):
+            cot_c[k].wait_recv()
+            piece = slice(n * (rows // 2), (n + 1) * (rows // 2))
+            cf_c.append(
+                remote(
+                    cotf.at[k, piece, :],
+                    cotf.at[3, piece, :],
+                    cf_s.at[n],
+                    cf_r.at[n],
+                    tensor_peer[3 - k],
+                )
+            )
 
     row_tile = tile_of(rows, 256)
     d_tile = tile_of(d, 512)
@@ -217,18 +262,18 @@
         to = dp_peer[j][0]
         g_c.append(
             (
-                remote(gd_snd.at[to], gd_ref.at[z, a], g_s.at[0, j], g_r.at[0, j], dp_peer[j]),
-                remote(gu_snd.at[to], gu_ref.at[z, a], g_s.at[1, j], g_r.at[1, j], dp_peer[j]),
-                remote(ids_ref, gid_ref.at[z], g_s.at[2, j], g_r.at[2, j], dp_peer[j]),
+                remote(gd_snd.at[to], gdf.at[z, a], g_s.at[0, j], g_r.at[0, j], dp_peer[j]),
+                remote(gu_snd.at[to], guf.at[z, a], g_s.at[1, j], g_r.at[1, j], dp_peer[j]),
+                remote(ids_v, gid.at[z], g_s.at[2, j], g_r.at[2, j], dp_peer[j]),
             )
         )
-    cp_gd = local(gd_snd.at[z], gd_ref.at[z, a], 5)
-    cp_gu = local(gu_snd.at[z], gu_ref.at[z, a], 6)
-    cp_id = local(ids_ref, gid_ref.at[z], 7)
+    cp_gd = local(gd_snd.at[z], gdf.at[z, a], 5)
+    cp_gu = local(gu_snd.at[z], guf.at[z, a], 6)
+    cp_id = local(ids_v, gid.at[z], 7)
     gr_c = [
         (
-            remote(gd_snd.at[z], gd_ref.at[z, a], gr_s.at[0, 0], gr_r.at[0, 0], partner),
-            remote(gu_snd.at[z], gu_ref.at[z, a], gr_s.at[1, 0], gr_r.at[1, 0], partner),
+            remote(gd_snd.at[z], gdf.at[z, a], gr_s.at[0, 0], gr_r.at[0, 0], partner),
+            remote(gu_snd.at[z], guf.at[z, a], gr_s.at[1, 0], gr_r.at[1, 0], partner),
         )
     ]
 
@@ -236,7 +281,11 @@
     o_c = [None] * num_tensor
 
     def relay(k):
-        w_c[k].wait_recv()
+        if k == far:
+            for j in range(1, num_dp):
+                wz_c[j].wait_recv()
+        else:
+            w_c[k].wait_recv()
         wr_c[k] = remote(
             wf.at[k, my_half, :], wf.at[k, my_half, :], wr_s.at[k], wr_r.at[k], partner
         )
@@ -254,8 +303,24 @@
         o_c[k] = remote(o_snd.at[k], o_rcv.at[k], o_s.at[k], o_r.at[k], tensor_peer[k])
         if k >= 2 and k + 1 < num_tensor:
             relay(k + 1)
-        cot_c[k].wait_recv()
+        if handed and k == far:
+            for copy in cf_c:
+                copy.wait_recv()
+        elif not handed:
+            cot_c[k].wait_recv()
         backward(k)
+
+    for j in range(1, num_dp):
+        for copy in g_c[j]:
+            copy.wait_recv()
+        source = lax.rem(z + num_dp - j, num_dp)
+        mine_d, mine_u = gdf.at[source, a], guf.at[source, a]
+        gr_c.append(
+            (
+                remote(mine_d, mine_d, gr_s.at[0, j], gr_r.at[0, j], partner),
+                remote(mine_u, mine_u, gr_s.at[1, j], gr_r.at[1, j], partner),
+            )
+        )
 
     for i in range(nb):
         blk = slice(i * BLOCK, (i + 1) * BLOCK)
@@ -268,17 +333,29 @@
     h_c = remote(h_fin, hid_ref.at[my_rows, :], fin_s.at[0], fin_r.at[0], partner)
     cp_h = local(h_fin, hid_ref.at[my_rows, :], 8)
 
-    for j in range(1, num_dp):
-        for copy in g_c[j]:
+    cp_gd.wait()
+    cp_gu.wait()
+    cp_id.wait()
+    for pair in gr_c:
+        for copy in pair:
             copy.wait_recv()
-        source = lax.rem(z + num_dp - j, num_dp)
-        mine_d, mine_u = gd_ref.at[source, a], gu_ref.at[source, a]
-        gr_c.append(
-            (
-                remote(mine_d, mine_d, gr_s.at[0, j], gr_r.at[0, j], partner),
-                remote(mine_u, mine_u, gr_s.at[1, j], gr_r.at[1, j], partner),
-            )
-        )
+    held = num_dp * 2 * nb * rk
+    width = principles * rk
+    grads_d = gdf[...].reshape(held, d)
+    grads_u = guf[...].reshape(held, c)
+    ids = gid[...].reshape(held, 128)
+    lane = lax.broadcasted_iota(jnp.int32, (held, 128), 1)
+    sub = lax.broadcasted_iota(jnp.int32, (held, 128), 0)
+    for part in range(width // 128):
+        to = slice(part * 128, (part + 1) * 128)
+        column = lane + part * 128
+        slot = (a * principles + column // rk).astype(jnp.float32)
+        hit = (ids == slot) & (column % rk == sub % rk)
+        select = jnp.where(hit, 1.0, 0.0).astype(jnp.float32).T.astype(jnp.bfloat16)
+        dmap_v[to, :] = jnp.dot(select, grads_d, preferred_element_type=jnp.float32)
+        umap_v[to, :] = jnp.dot(select, grads_u, preferred_element_type=jnp.float32)
+    cp_dm = local(dmap_v, dmap_ref, 10)
+    cp_um = local(umap_v, umap_ref, 11)
 
     for k in range(1, num_tensor):
         o_c[k].wait_recv()
@@ -291,22 +368,26 @@
     of_c = remote(o_fin, out_ref.at[my_rows, :], fin_s.at[1], fin_r.at[1], partner)
     cp_o = local(o_fin, out_ref.at[my_rows, :], 9)
 
-    for copy in (cp_gd, cp_gu, cp_id, cp_h, cp_o):
+    for copy in (cp_h, cp_o, cp_dm, cp_um):
         copy.wait()
     for k in range(1, num_tensor):
-        cot_c[k].wait_send()
+        if cot_c[k] is not None:
+            cot_c[k].wait_send()
         w_c[k].wait_send()
         rk_c[k].wait_send()
         wr_c[k].wait_send()
         o_c[k].wait_send()
+    for copy in cf_c:
+        copy.wait_send()
     a_c.wait_send()
     b_c.wait_send()
     for j in range(1, num_dp):
         for copy in g_c[j]:
             copy.wait_send()
+        wz_c[j].wait_send()
     for pair in gr_c:
         for copy in pair:
-            copy.wait()
+            copy.wait_send()
     h_c.wait()
     of_c.wait()
 
@@ -327,28 +408,21 @@
     principles, rank = adapter_down_weight.shape[:2]
     blocks = all_rows // BLOCK
     rows, nb, rk = all_rows // 2, blocks // 2, rank // num_dp
-    core = lax.axis_index("adapter")
-    local_pick = principle_per_block - core * principles
-    owned = ((local_pick >= 0) & (local_pick < principles)).astype(jnp.float32)
-    pick = jnp.clip(local_pick, 0, principles - 1)
-    ids = jnp.broadcast_to(principle_per_block.astype(jnp.float32)[:, None], (blocks, 128))
-
     bf, f32 = jnp.bfloat16, jnp.float32
     hbm = pl.BlockSpec(memory_space=pl.ANY)
     smem = pl.BlockSpec(memory_space=pltpu.SMEM)
     dma = pltpu.SemaphoreType.DMA
     T, Z = num_tensor, num_dp
-    out, hidden, gd, gu, gid = pl.pallas_call(
+    out, hidden, dmap, umap = pl.pallas_call(
         functools.partial(kernel, T, Z),
         out_shape=(
             jax.ShapeDtypeStruct((all_rows, c), bf),
             jax.ShapeDtypeStruct((all_rows, d), bf),
-            jax.ShapeDtypeStruct((Z, 2, nb * rk, d), bf),
-            jax.ShapeDtypeStruct((Z, 2, nb * rk, c), bf),
-            jax.ShapeDtypeStruct((Z, blocks, 128), f32),
+            jax.ShapeDtypeStruct((principles * rk, d), f32),
+            jax.ShapeDtypeStruct((principles * rk, c), f32),
         ),
-        in_specs=[hbm] * 5 + [smem] * 3 + [hbm],
-        out_specs=[hbm] * 5,
+        in_specs=[hbm] * 5 + [smem] * 2,
+        out_specs=[hbm] * 4,
         scratch_shapes=[
             pltpu.VMEM((rows, d), bf),
             pltpu.VMEM((T, d, c), bf),
@@ -366,17 +440,27 @@
             pltpu.VMEM((rows, 2 * rank), bf),
             pltpu.VMEM((Z, nb * rk, d), bf),
             pltpu.VMEM((Z, nb * rk, c), bf),
+            pltpu.VMEM((2 * nb * rk, 128), f32),
+            pltpu.VMEM((Z, 2, nb * rk, d), bf),
+            pltpu.VMEM((Z, 2, nb * rk, c), bf),
+            pltpu.VMEM((Z, 2 * nb * rk, 128), f32),
+            pltpu.VMEM((principles * rk, d), f32),
+            pltpu.VMEM((principles * rk, c), f32),
             pltpu.VMEM((rows, d), f32),
             pltpu.VMEM((rows, c), f32),
             pltpu.VMEM((T, rows, c), bf),
             pltpu.VMEM((T, rows, c), bf),
             pltpu.VMEM((rows, c), bf),
             pltpu.VMEM((rows, d), bf),
-            dma((10,)),
-            dma((T,)),
-            dma((T,)),
-            dma((T,)),
-            dma((T,)),
+            dma((12,)),
+            dma((T,)),
+            dma((T,)),
+            dma((2,)),
+            dma((2,)),
+            dma((T,)),
+            dma((T,)),
+            dma((Z,)),
+            dma((Z,)),
             dma((T,)),
             dma((T,)),
             dma((2,)),
@@ -404,18 +488,10 @@
         adapter_down_weight,
         adapter_up_weight,
         output_cotangent,
-        pick,
-        owned,
+        principle_per_block,
         live_block_rows,
-        ids,
     )
-    slots = core * principles + jnp.arange(principles, dtype=jnp.int32)
-    chosen = (slots[:, None].astype(f32) == gid[:, :, 0].reshape(1, -1)).astype(bf)
-    gd = gd.reshape(Z * blocks, rk, d)
-    gu = gu.reshape(Z * blocks, rk, c)
-    down_map_gradient = jnp.einsum("pb,bkd->pkd", chosen, gd, preferred_element_type=f32)
-    up_map_gradient = jnp.einsum("pb,bkd->pkd", chosen, gu, preferred_element_type=f32)
-    return out, hidden, down_map_gradient, up_map_gradient
+    return out, hidden, dmap.reshape(principles, rk, d), umap.reshape(principles, rk, c)
 
 
 def solution(mesh):

time: 135 us -> 97.9 us (0.73)
  Pallas kernels: 116 us -> 86.9 us
  matrix products: 4.97 us -> 0 us
  other arithmetic: 2.42 us -> 0 us
    pallas_call x1, Pallas kernels: 116 us -> 86.9 us  [on_device(): pl.pallas_call(functools.partial(kernel, T, Z), out_shape=(jax.ShapeDtype...]
    dot_general x2 -> x0, matrix products: 4.97 us -> none  [the longest x1 4.48 us: on_device(): jnp.einsum('pb,bkd->pkd', chosen, gd, preferred_element_type=f32)]
    convert_element_type x3 -> x0, other arithmetic: 2.42 us -> none  [the longest x1 1.25 us: on_device(): principle_per_block.astype(jnp.float32)[:, None]]
    unnamed x10 -> x8, local copies, waits for them, and re-layouts: 9.02 us -> 10.2 us
where the time goes in v2:
time: 97.9 us; the launch traced here: 97.7 us
  Pallas kernels  86.9 us (89%)
  local copies, waits for them, and re-layouts  10.2 us (10%)
    pallas_call x1, Pallas kernels, on_device(): pl.pallas_call(functools.partial(kernel, T, Z), out_shape=(jax.ShapeDtype...  86.9 us
    unnamed x8, local copies, waits for them, and re-layouts  10.2 us

profile of v2, /device:TPU:0, one launch (start us, length us, event | category | flops | bytes accessed | tf_op | source)
XLA Modules:
  0.0 97.7 jit_solution(16300764218123636308)
XLA Ops:
  0.6 86.9 %shard_map.102 = (bf16[1024,512]{1,0:T(8,128)(2,1)}, bf16[1024,2048]{1,0:T(8,128)(2,1)}, f32[512,2048]{1,0:T(8,128)}, f32[512,512]{1,0:T(8,128)}) custom-call(bf16[1024,2048]{1,0:T(8,128)(2,1)} %tok_ref.1, bf16[8192,512]{1,0:T(8,128)(2,1)} %w_ref.1, bf16[32,64,2048]{2,1,0:T(8,128)(2,1)} %down_ref.1, bf16[32,64,512]{2,1,0:T(8,128)(2,1)} %up_ref.1, ...), custom_call_target="tpu_custom_call" | custom-call | flops 8589934592 | bytes 33554432 | tf_op jit(solution)/shard_map/pallas_call | solution.py:416
  87.5 2.3 %copy.15 = bf16[1024,512]{1,0:T(8,128)(2,1)} copy(bf16[1024,512]{1,0:T(8,128)(2,1)} %get-tuple-element.16) | data formatting | bytes 2097152
  89.8 0.0 copy-start
  89.8 4.9 %copy.16 = bf16[1024,2048]{1,0:T(8,128)(2,1)} copy(bf16[1024,2048]{1,0:T(8,128)(2,1)} %get-tuple-element.17) | data formatting | bytes 8388608
  94.7 0.0 copy-done
  94.7 0.0 copy-start.1
  94.7 2.0 %copy.17 = f32[32,16,2048]{2,1,0:T(8,128)} copy(f32[32,16,2048]{2,1,0:T(8,128)S(1)} %bitcast.2) | data formatting | bytes 8388608
  96.7 0.0 copy-done.1
  96.7 1.0 copy.18
Async XLA Ops:
  89.8 4.9 %copy-start = (f32[512,2048]{1,0:T(8,128)S(1)}, f32[512,2048]{1,0:T(8,128)}, u32[]{:S(2)}) copy-start(f32[512,2048]{1,0:T(8,128)} %get-tuple-element.10) | copy-start | bytes 12582916
  94.7 2.0 %copy-start.1 = (f32[512,512]{1,0:T(8,128)S(1)}, f32[512,512]{1,0:T(8,128)}, u32[]{:S(2)}) copy-start(f32[512,512]{1,0:T(8,128)} %get-tuple-element.11) | copy-start | bytes 3145732

commit v3 on v2

--- a/solution.py
+++ b/solution.py
@@ -58,14 +58,10 @@
     gdf,
     guf,
     gid,
-    dmap_v,
-    umap_v,
     acc,
     o_zero,
     o_snd,
     o_rcv,
-    o_fin,
-    h_fin,
     loc_sem,
     cot_s,
     cot_r,
@@ -267,9 +263,9 @@
                 remote(ids_v, gid.at[z], g_s.at[2, j], g_r.at[2, j], dp_peer[j]),
             )
         )
-    cp_gd = local(gd_snd.at[z], gdf.at[z, a], 5)
-    cp_gu = local(gu_snd.at[z], guf.at[z, a], 6)
-    cp_id = local(ids_v, gid.at[z], 7)
+    cp_gd = local(gd_snd.at[z], gdf.at[z, a], 1)
+    cp_gu = local(gu_snd.at[z], guf.at[z, a], 2)
+    cp_id = local(ids_v, gid.at[z], 0)
     gr_c = [
         (
             remote(gd_snd.at[z], gdf.at[z, a], gr_s.at[0, 0], gr_r.at[0, 0], partner),
@@ -327,11 +323,12 @@
         low_b = rank_v[blk, :rank]
         back_b = rank_v[blk, rank:]
         term = jnp.dot(back_b, a_own[i], preferred_element_type=jnp.float32)
-        h_fin[blk, :] = (acc[blk, :] + ADAPTER_SCALE * term).astype(jnp.bfloat16)
+        at = pl.ds(pl.multiple_of(a * rows + i * BLOCK, BLOCK), BLOCK)
+        hid_ref[at, :] = (acc[blk, :] + ADAPTER_SCALE * term).astype(jnp.bfloat16)
         o_term = jnp.dot(low_b, b_own[i], preferred_element_type=jnp.float32)
         o_zero[blk, :] = o_zero[blk, :] + ADAPTER_SCALE * o_term
-    h_c = remote(h_fin, hid_ref.at[my_rows, :], fin_s.at[0], fin_r.at[0], partner)
-    cp_h = local(h_fin, hid_ref.at[my_rows, :], 8)
+    mine = hid_ref.at[my_rows, :]
+    h_c = remote(mine, mine, fin_s.at[0], fin_r.at[0], partner)
 
     cp_gd.wait()
     cp_gu.wait()
@@ -347,15 +344,15 @@
     lane = lax.broadcasted_iota(jnp.int32, (held, 128), 1)
     sub = lax.broadcasted_iota(jnp.int32, (held, 128), 0)
     for part in range(width // 128):
-        to = slice(part * 128, (part + 1) * 128)
+        to = slice(part * 128 // rk, (part + 1) * 128 // rk)
         column = lane + part * 128
         slot = (a * principles + column // rk).astype(jnp.float32)
         hit = (ids == slot) & (column % rk == sub % rk)
         select = jnp.where(hit, 1.0, 0.0).astype(jnp.float32).T.astype(jnp.bfloat16)
-        dmap_v[to, :] = jnp.dot(select, grads_d, preferred_element_type=jnp.float32)
-        umap_v[to, :] = jnp.dot(select, grads_u, preferred_element_type=jnp.float32)
-    cp_dm = local(dmap_v, dmap_ref, 10)
-    cp_um = local(umap_v, umap_ref, 11)
+        down = jnp.dot(select, grads_d, preferred_element_type=jnp.float32)
+        dmap_ref[to] = down.reshape(128 // rk, rk, d)
+        up = jnp.dot(select, grads_u, preferred_element_type=jnp.float32)
+        umap_ref[to] = up.reshape(128 // rk, rk, c)
 
     for k in range(1, num_tensor):
         o_c[k].wait_recv()
@@ -364,12 +361,11 @@
         total = o_zero[blk, :]
         for k in range(1, num_tensor):
             total = total + o_rcv[k, blk, :].astype(jnp.float32)
-        o_fin[blk, :] = total.astype(jnp.bfloat16)
-    of_c = remote(o_fin, out_ref.at[my_rows, :], fin_s.at[1], fin_r.at[1], partner)
-    cp_o = local(o_fin, out_ref.at[my_rows, :], 9)
-
-    for copy in (cp_h, cp_o, cp_dm, cp_um):
-        copy.wait()
+        at = pl.ds(pl.multiple_of(a * rows + i * BLOCK, BLOCK), BLOCK)
+        out_ref[at, :] = total.astype(jnp.bfloat16)
+    mine = out_ref.at[my_rows, :]
+    of_c = remote(mine, mine, fin_s.at[1], fin_r.at[1], partner)
+
     for k in range(1, num_tensor):
         if cot_c[k] is not None:
             cot_c[k].wait_send()
@@ -392,6 +388,14 @@
     of_c.wait()
 
 
+def write_out(*refs):
+    copies = [pltpu.make_async_copy(refs[n], refs[4 + n], refs[8].at[n]) for n in range(4)]
+    for copy in copies:
+        copy.start()
+    for copy in copies:
+        copy.wait()
+
+
 def on_device(
     num_tensor,
     num_dp,
@@ -410,19 +414,20 @@
     rows, nb, rk = all_rows // 2, blocks // 2, rank // num_dp
     bf, f32 = jnp.bfloat16, jnp.float32
     hbm = pl.BlockSpec(memory_space=pl.ANY)
+    vmem = pl.BlockSpec(memory_space=pltpu.VMEM)
     smem = pl.BlockSpec(memory_space=pltpu.SMEM)
     dma = pltpu.SemaphoreType.DMA
     T, Z = num_tensor, num_dp
-    out, hidden, dmap, umap = pl.pallas_call(
+    results = pl.pallas_call(
         functools.partial(kernel, T, Z),
         out_shape=(
-            jax.ShapeDtypeStruct((all_rows, c), bf),
-            jax.ShapeDtypeStruct((all_rows, d), bf),
-            jax.ShapeDtypeStruct((principles * rk, d), f32),
-            jax.ShapeDtypeStruct((principles * rk, c), f32),
+            pltpu.VMEM((all_rows, c), bf),
+            pltpu.VMEM((all_rows, d), bf),
+            pltpu.VMEM((principles, rk, d), f32),
+            pltpu.VMEM((principles, rk, c), f32),
         ),
         in_specs=[hbm] * 5 + [smem] * 2,
-        out_specs=[hbm] * 4,
+        out_specs=[vmem] * 4,
         scratch_shapes=[
             pltpu.VMEM((rows, d), bf),
             pltpu.VMEM((T, d, c), bf),
@@ -444,15 +449,11 @@
             pltpu.VMEM((Z, 2, nb * rk, d), bf),
             pltpu.VMEM((Z, 2, nb * rk, c), bf),
             pltpu.VMEM((Z, 2 * nb * rk, 128), f32),
-            pltpu.VMEM((principles * rk, d), f32),
-            pltpu.VMEM((principles * rk, c), f32),
             pltpu.VMEM((rows, d), f32),
             pltpu.VMEM((rows, c), f32),
             pltpu.VMEM((T, rows, c), bf),
             pltpu.VMEM((T, rows, c), bf),
-            pltpu.VMEM((rows, c), bf),
-            pltpu.VMEM((rows, d), bf),
-            dma((12,)),
+            dma((5,)),
             dma((T,)),
             dma((T,)),
             dma((2,)),
@@ -477,7 +478,7 @@
             dma((2,)),
         ],
         compiler_params=pltpu.CompilerParams(
-            collective_id=0, has_side_effects=True, vmem_limit_bytes=56 * 1024 * 1024
+            collective_id=0, has_side_effects=True, vmem_limit_bytes=46 * 1024 * 1024
         ),
         cost_estimate=pl.CostEstimate(
             flops=4 * rows * d * c * T, bytes_accessed=8 * d * c * T, transcendentals=0
@@ -491,7 +492,13 @@
         principle_per_block,
         live_block_rows,
     )
-    return out, hidden, dmap.reshape(principles, rk, d), umap.reshape(principles, rk, c)
+    return pl.pallas_call(
+        write_out,
+        out_shape=tuple(jax.ShapeDtypeStruct(r.shape, r.dtype) for r in results),
+        in_specs=[vmem] * 4,
+        out_specs=[hbm] * 4,
+        scratch_shapes=[dma((4,))],
+    )(*results)
 
 
 def solution(mesh):

time: 97.9 us -> 101 us (1.032)
  Pallas kernels: 86.9 us -> 94.6 us
  local copies, waits for them, and re-layouts: 10.2 us -> 5.88 us
    pallas_call x1 -> x2, Pallas kernels: 86.9 us -> 94.6 us  [the longest x1 86.7 us: on_device(): pl.pallas_call(functools.partial(kernel, T, Z), out_shape=(pltpu.VMEM((al...]
    unnamed x8, local copies, waits for them, and re-layouts: 10.2 us -> 5.88 us
where the time goes in v3:
time: 101 us
  Pallas kernels  94.6 us (94%)
  local copies, waits for them, and re-layouts  5.88 us (6%)
    pallas_call x1, Pallas kernels, on_device(): pl.pallas_call(functools.partial(kernel, T, Z), out_shape=(pltpu.VMEM((al...  86.7 us
    pallas_call x1, Pallas kernels, on_device(): pl.pallas_call(write_out, out_shape=tuple((jax.ShapeDtypeStruct(r.shape,...  7.98 us
    unnamed x8, local copies, waits for them, and re-layouts  5.88 us

profile of v3, /device:TPU:0, one launch (start us, length us, event | category | flops | bytes accessed | tf_op | source)
XLA Modules:
  0.0 101.2 jit_solution(4104284255544915543)
XLA Ops:
  0.6 86.7 %shard_map.102 = (bf16[1024,512]{1,0:T(8,128)(2,1)S(1)}, bf16[1024,2048]{1,0:T(8,128)(2,1)S(1)}, f32[32,16,2048]{2,1,0:T(8,128)S(1)}, f32[32,16,512]{2,1,0:T(8,128)S(1)}) custom-call(bf16[1024,2048]{1,0:T(8,128)(2,1)} %tok_ref.1, bf16[8192,512]{1,0:T(8,128)(2,1)} %w_ref.1, bf16[32,64,2048]{2,1,0:T(8,128)(2,1)} %down_ref.1, bf16[32,64,512]{2,1,0:T(8,128)(2,1)} %up_ref.1, ...), custom_call_target="tpu_custom_call" | custom-call | flops 8589934592 | bytes 33554432 | tf_op jit(solution)/shard_map/pallas_call | solution.py:421
  87.3 0.0 copy-start
  87.3 1.9 %copy-done = bf16[1024,2048]{1,0:T(8,128)(2,1)} copy-done((bf16[1024,2048]{1,0:T(8,128)(2,1)}, bf16[1024,2048]{1,0:T(8,128)(2,1)S(1)}, u32[]{:S(2)}) %copy-start) | copy-done | bytes 4194328
  89.2 0.0 copy-start.1
  89.2 2.0 %copy-done.1 = f32[32,16,2048]{2,1,0:T(8,128)} copy-done((f32[32,16,2048]{2,1,0:T(8,128)}, f32[32,16,2048]{2,1,0:T(8,128)S(1)}, u32[]{:S(2)}) %copy-start.1) | copy-done | bytes 4194328
  91.2 0.0 copy-start.2
  91.2 1.0 %copy-done.2 = bf16[1024,512]{1,0:T(8,128)(2,1)} copy-done((bf16[1024,512]{1,0:T(8,128)(2,1)}, bf16[1024,512]{1,0:T(8,128)(2,1)S(1)}, u32[]{:S(2)}) %copy-start.2) | copy-done | bytes 1048600
  92.3 0.0 copy-start.3
  92.3 0.9 copy-done.3
  93.2 8.0 %shard_map.103 = (bf16[1024,512]{1,0:T(8,128)(2,1)}, bf16[1024,2048]{1,0:T(8,128)(2,1)}, f32[32,16,2048]{2,1,0:T(8,128)}, f32[32,16,512]{2,1,0:T(8,128)}) custom-call(bf16[1024,512]{1,0:T(8,128)(2,1)} %copy-done.2, bf16[1024,2048]{1,0:T(8,128)(2,1)} %copy-done, f32[32,16,2048]{2,1,0:T(8,128)} %copy-done.1, f32[32,16,512]{2,1,0:T(8,128)} %copy-done.3), custom_call_target="tpu_custom_call" | custom-call | tf_op jit(solution)/shard_map/pallas_call | solution.py:495
Async XLA Ops:
  87.3 1.9 %copy-start = (bf16[1024,2048]{1,0:T(8,128)(2,1)}, bf16[1024,2048]{1,0:T(8,128)(2,1)S(1)}, u32[]{:S(2)}) copy-start(bf16[1024,2048]{1,0:T(8,128)(2,1)S(1)} %get-tuple-element.9.refs_1_) | copy-start | bytes 12582916
  89.2 2.0 %copy-start.1 = (f32[32,16,2048]{2,1,0:T(8,128)}, f32[32,16,2048]{2,1,0:T(8,128)S(1)}, u32[]{:S(2)}) copy-start(f32[32,16,2048]{2,1,0:T(8,128)S(1)} %get-tuple-element.10.refs_2_) | copy-start | bytes 12582916
  91.2 1.0 %copy-start.2 = (bf16[1024,512]{1,0:T(8,128)(2,1)}, bf16[1024,512]{1,0:T(8,128)(2,1)S(1)}, u32[]{:S(2)}) copy-start(bf16[1024,512]{1,0:T(8,128)(2,1)S(1)} %get-tuple-element.8.refs_0_) | copy-start | bytes 3145732
  92.3 1.0 copy-start.3

commit v4 on v3

--- a/solution.py
+++ b/solution.py
@@ -498,6 +498,7 @@
         in_specs=[vmem] * 4,
         out_specs=[hbm] * 4,
         scratch_shapes=[dma((4,))],
+        compiler_params=pltpu.CompilerParams(vmem_limit_bytes=1024 * 1024),
     )(*results)
 
 

time: 101 us -> 91.5 us (0.906)
  local copies, waits for them, and re-layouts: 5.88 us -> 0 us
  Pallas kernels: 94.6 us -> 90.7 us
    unnamed x8 -> x0, local copies, waits for them, and re-layouts: 5.88 us -> none
    pallas_call x1, Pallas kernels: 7.98 us -> 3.99 us  [on_device(): pl.pallas_call(write_out, out_shape=tuple((jax.ShapeDtypeStruct(r.shape,...]
where the time goes in v4:
time: 91.5 us; the launch traced here: 91.3 us
  Pallas kernels  90.7 us (99%)
    pallas_call x1, Pallas kernels, on_device(): pl.pallas_call(functools.partial(kernel, T, Z), out_shape=(pltpu.VMEM((al...  86.7 us
    pallas_call x1, Pallas kernels, on_device(): pl.pallas_call(write_out, out_shape=tuple((jax.ShapeDtypeStruct(r.shape,...  3.99 us

profile of v4, /device:TPU:0, one launch (start us, length us, event | category | flops | bytes accessed | tf_op | source)
XLA Modules:
  0.0 91.3 jit_solution(6099440376115431482)
XLA Ops:
  0.6 86.7 %shard_map.102 = (bf16[1024,512]{1,0:T(8,128)(2,1)S(1)}, bf16[1024,2048]{1,0:T(8,128)(2,1)S(1)}, f32[32,16,2048]{2,1,0:T(8,128)S(1)}, f32[32,16,512]{2,1,0:T(8,128)S(1)}) custom-call(bf16[1024,2048]{1,0:T(8,128)(2,1)} %tok_ref.1, bf16[8192,512]{1,0:T(8,128)(2,1)} %w_ref.1, bf16[32,64,2048]{2,1,0:T(8,128)(2,1)} %down_ref.1, bf16[32,64,512]{2,1,0:T(8,128)(2,1)} %up_ref.1, ...), custom_call_target="tpu_custom_call" | custom-call | flops 8589934592 | bytes 33554432 | tf_op jit(solution)/shard_map/pallas_call | solution.py:421
  87.3 4.0 %shard_map.103 = (bf16[1024,512]{1,0:T(8,128)(2,1)}, bf16[1024,2048]{1,0:T(8,128)(2,1)}, f32[32,16,2048]{2,1,0:T(8,128)}, f32[32,16,512]{2,1,0:T(8,128)}) custom-call(bf16[1024,512]{1,0:T(8,128)(2,1)S(1)} %get-tuple-element.8.refs_0_, bf16[1024,2048]{1,0:T(8,128)(2,1)S(1)} %get-tuple-element.9.refs_1_, f32[32,16,2048]{2,1,0:T(8,128)S(1)} %get-tuple-element.10.refs_2_, ...), custom_call_target="tpu_custom_call" | custom-call | tf_op jit(solution)/shard_map/pallas_call | solution.py:495
